TPU v7x, 256 devices: a whole 4x4x8 slice. The times are simulated.
256 devices in a mesh: group: 8 (over y, core), tile: 32 (over z, x).
Axes of the slice: x: 4, y: 4, z: 8, core: 2. Of those that a mesh axis runs over, the one named last changes fastest.
Arguments:
- embeddings: bfloat16 [8, 16384, 768], P('group', 'tile'), may hold values from -30 to 30
- cluster_ids: int32 [8, 16384], P('group', 'tile'), may hold values from 0 to 7, never falling along the last dimension, each value on 1 to 12288 neighbouring positions
Outputs:
- duplicate_score: float32 [8, 16384], P('group', 'tile')
Inputs may be any that keep to these rules, and one draw needn't show every extreme that they name: `cluster_ids`: within each cluster group the cluster numbers never fall along the member order; each cluster has 1 to 12288 members, and some cluster has exactly that many.
All inputs are finite; a program needn't handle non-finite values.
Results may differ from a plain program's by a relative error of at most 0.0005.
Values may be sent and summed in bfloat16 or wider, within the bound.
A program may use at most 128 MiB of HBM per device.

v0:
```python
import math

import jax
import jax.numpy as jnp
from jax import lax
from jax.sharding import PartitionSpec as P


def local(embeddings, cluster_ids):
    length = embeddings.shape[1]
    width = embeddings.shape[2]
    groups = lax.axis_size("group")
    portion = length // groups
    values = embeddings[0].astype(jnp.float32)
    unit = (values / jnp.sqrt(jnp.sum(values * values, axis=1, keepdims=True) + 1e-06)).astype(
        jnp.bfloat16
    )
    routed = lax.all_to_all(
        unit.reshape(groups, portion, width), "group", split_axis=0, concat_axis=0, tiled=True
    ).reshape(length, width)
    own_ids = cluster_ids[0]
    wire_ids = own_ids.astype(jnp.bfloat16)
    mine = lax.axis_index("tile")
    own_index = mine * length + jnp.arange(length, dtype=jnp.int32)

    def scored(piece, piece_ids, first):
        scores = jnp.einsum("rd,cd->rc", routed, piece, preferred_element_type=jnp.float32)
        other_ids = piece_ids.astype(jnp.int32)
        other_index = first + jnp.arange(piece.shape[0], dtype=jnp.int32)
        keep = (own_ids[:, None] == other_ids[None, :]) & (
            own_index[:, None] != other_index[None, :]
        )
        return jnp.where(keep, scores, -1.0)

    def unchanged(state):
        return state

    start_best = jnp.full((length,), -1.0, jnp.float32)
    piece = lax.all_gather(routed, "tile", axis=0, tiled=True)
    piece_ids = lax.all_gather(wire_ids, "tile", axis=0, tiled=True)
    amount = piece.shape[0]
    step_rows = math.gcd(amount, length)
    steps = amount // step_rows
    items = (
        piece.reshape(steps, step_rows, width),
        piece_ids.reshape(steps, step_rows),
        step_rows * jnp.arange(steps, dtype=jnp.int32),
    )

    def visit(current, item):
        block, block_ids, block_first = item

        def update(state):
            return jnp.maximum(state, jnp.max(scored(block, block_ids, block_first), axis=1))

        return (lax.cond(jnp.bool_(True), update, unchanged, current), None)

    result, _ = lax.scan(visit, start_best, items)
    answer = lax.all_to_all(
        result.reshape(groups, portion), "group", split_axis=0, concat_axis=0, tiled=True
    )
    return answer.reshape(1, length)


def solution(mesh):
    in_specs = (P("group", "tile", None), P("group", "tile"))
    out_specs = P("group", "tile")
    return jax.shard_map(local, mesh=mesh, in_specs=in_specs, out_specs=out_specs, check_vma=False)
```

profile of v0, /device:TPU:24, one launch (start us, length us, event | category | flops | bytes accessed | tf_op | source)
XLA Modules:
  0.0 332.4 jit_solution(8767697284310622218)
XLA Ops:
  9.4 16.2 %all_to_all.14 = bf16[8,64,768]{2,1,0:T(8,128)(2,1)} all-to-all(bf16[8,64,768]{2,1,0:T(8,128)(2,1)S(1)} %divide_convert_fusion), channel_id=1, replica_groups=mesh['group'=8,'tile'=32] {'group'}, dimensions={0} | all-to-all | bytes 1572864 | tf_op jit(solution)/shard_map/all_to_all | solution.py:18
  25.7 51.4 %all-gather = bf16[1,16384]{1,0:T(2,128)(2,1)S(1)} all-gather(bf16[1,512]{1,0:T(2,128)(2,1)S(1)} %convert_element_type.22), channel_id=2, replica_groups=mesh['group'=8,'tile'=32] {'tile'}, dimensions={1}, use_global_device_ids=true | all-gather | bytes 33792 | tf_op jit(solution)/shard_map/all_gather | solution.py:40
  77.3 134.5 %all-gather.3.cloned.1.call-done = bf16[16384,768]{1,0:T(8,128)(2,1)} async-done(((bf16[512,768]{1,0:T(8,128)(2,1)}), bf16[16384,768]{1,0:T(8,128)(2,1)}) %all-gather.3.cloned.1.call-update) | async-done | bytes 25165840 | tf_op jit(solution)/shard_map/all_gather | solution.py:39
  211.9 104.0 %while.11 = (s32[]{:T(128)}, f32[512]{0:T(512)S(1)}, s32[1,512]{1,0:T(1,128)S(1)}, bf16[32,512]{1,0:T(8,128)(2,1)S(1)}, s32[32]{0:T(128)S(1)}, /*index=5*/bf16[3...) while((s32[]{:T(128)}, f32[512]{0:T(512)S(1)}, ...), condition=%wide.region_3.4_spmd.clone, body=%wide.region_1.3_spmd.clone.sunk | while | flops 403965952 | bytes 1596563 | solution.py:58
  213.1 2.0 fusion.13
  216.3 2.0 fusion.13
  219.6 2.0 fusion.13
  222.8 2.0 fusion.13
  229.3 2.0 fusion.13
  232.6 2.0 fusion.13
  235.8 2.0 fusion.13
  242.3 2.0 fusion.13
  245.6 2.0 fusion.13
  248.8 2.0 fusion.13
  258.6 2.0 fusion.13
  265.1 2.0 fusion.13
  271.6 2.0 fusion.13
  278.1 2.0 fusion.13
  284.6 2.0 fusion.13
  291.1 2.0 fusion.13
  297.6 2.0 fusion.13
  304.1 2.0 fusion.13
  310.6 2.0 fusion.13
  316.0 7.8 %all_to_all.15 = f32[8,1,64]{2,1,0:T(1,128)S(1)} all-to-all(f32[8,1,64]{2,1,0:T(1,128)S(1)} %all_to_all.10), channel_id=1, replica_groups=mesh['group'=8,'tile'=32] {'group'}, dimensions={0} | all-to-all | bytes 4096 | tf_op jit(solution)/shard_map/all_to_all | solution.py:59
  (158 shorter events, 69.2 us)
Async XLA Ops:
  6.5 205.3 %all-gather.3.cloned.1.call-start = ((), (), s32[]{:S(2)}) async-start(), calls=%async_computation.2 | async-start | bytes 25952256 | tf_op jit(solution)/shard_map/all_gather | solution.py:39
  9.4 16.3 %copy-start = (s32[1,512]{1,0:T(1,128)S(1)}, s32[1,512]{1,0:T(1,128)}, u32[]{:S(2)}) copy-start(s32[1,512]{1,0:T(1,128)} %param.5) | copy-start | bytes 6148
Sparse Core Ops, SparseCore 0:
  25.8 186.0 all-gather.2
where the time goes:
time: 336 us; the launch traced here: 332 us
  waiting for transfers between devices  135 us (40%)
  blocking collectives  75.4 us (22%)
  matrix products  64.7 us (19%)
  other arithmetic  22.7 us (7%)
  local copies, waits for them, and re-layouts  20.2 us (6%)
  between operations  13.5 us (4%)
    all_gather x1, waiting for transfers between devices, local(): piece = lax.all_gather(routed, 'tile', axis=0, tiled=True)  135 us
    dot_general x32, matrix products, scored(): jnp.einsum('rd,cd->rc', routed, piece, preferred_element_type=jnp.float32)  64.7 us
    all_gather x1, blocking collectives, local(): piece_ids = lax.all_gather(wire_ids, 'tile', axis=0, tiled=True)  51.4 us
    dynamic_slice x32, local copies, waits for them, and re-layouts, local(): result, _ = lax.scan(visit, start_best, items)  18.8 us
    add x32, other arithmetic, local(): own_index = mine * length + jnp.arange(length, dtype=jnp.int32)  18.3 us
    all_to_all x1, blocking collectives, local(): lax.all_to_all(unit.reshape(groups, portion, width), 'group', split_axis=...  16.2 us
    all_to_all x1, blocking collectives, local(): lax.all_to_all(result.reshape(groups, portion), 'group', split_axis=0, co...  7.77 us
  transfers between devices with their start and end apart: 1, of which 1 were waited for; matrix products, arithmetic and copies ran while one was open for 0% of the time, Pallas kernels for 0%

commit v1 on v0

v1 whole, which is shorter than its diff:
```python
import functools

import jax
import jax.numpy as jnp
from jax import lax
from jax.experimental import pallas as pl
from jax.experimental.pallas import tpu as pltpu
from jax.sharding import PartitionSpec as P

MESH = pl.DeviceIdType.MESH
D = 768
ROWS = 512
PIECE = 64

COVER = ((0, 0), (0, 1), (0, -1), (1, -1), (-1, -1), (2, -1))
SIBLING = (0, 1, 3)
OFFSETS = (0, 1, -1, 2, -2, 3, -3, 4)
STEPS = ((0, 1), (1, 1), (2, 2), (4, 2), (6, 2))
SENT = ((1, 2), (3, 4), (5, 6), (7,), (), ())
FULL = ((0, 2), (0, 3), (0, 4), (0, 5), (2, 3), (1, 6), (2, 6), (4, 6), (5, 6), (4, 8), (5, 8))
HALF = ((1, 2, 0), (1, 3, 0), (1, 4, 0), (1, 5, 0), (2, 5, 1), (0, 6, 2), (3, 6, 2), (1, 7, 2), (3, 8, 2))


def pick(n, table):
    value = jnp.int32(table[0])
    for at in range(1, len(table)):
        value = jnp.where(n == at, jnp.int32(table[at]), value)
    return value


def kernel(
    x_ref, bound_ref, out_ref,
    unit, slots, idr, idc, rowacc, colacc, res, inb, near, obuf,
    z_send, z_recv, t_send, t_recv, r_send, r_recv, o_send, o_recv,
):
    group = lax.axis_index("group")
    tile = lax.axis_index("tile")
    y, c = group // 2, group % 2
    z, x = tile // 4, tile % 4
    flip = c == 1
    u = jnp.where(flip, y, x)
    v = jnp.where(flip, x, y)

    def chip(du, dv, other):
        nu, nv = (u + du + 4) % 4, (v + dv + 4) % 4
        nx = jnp.where(flip, nv, nu)
        ny = jnp.where(flip, nu, nv)
        nc = 1 - c if other else c
        return {"group": ny * 2 + nc, "tile": z * 4 + nx}

    def plane(dz):
        return {"group": group, "tile": ((z + dz + 8) % 8) * 4 + x}

    barrier = pltpu.get_barrier_semaphore()
    partners = [plane(o) for o in range(1, 8)]
    partners += [chip(a, b, False) for a, b in ((0, 1), (0, -1), (1, 0), (-1, 0), (1, -1), (-1, 1), (-1, -1), (1, 1), (2, -1), (2, 1))]
    partners += [chip(a, b, True) for a, b in ((0, 0), (1, 0), (0, -1), (-1, 1))]
    for partner in partners:
        pl.semaphore_signal(barrier, inc=1, device_id=partner, device_id_type=MESH)

    def normalize(p):
        k = (z - OFFSETS[p] + 8) % 8
        values = x_ref[0, pl.ds(pl.multiple_of(k * PIECE, PIECE), PIECE), :].astype(jnp.float32)
        total = jnp.sum(values * values, axis=1, keepdims=True) + 1e-06
        return (values * (1.0 / jnp.sqrt(total))).astype(jnp.bfloat16)

    slots[0, 0:PIECE, :] = normalize(0)
    for p in range(1, 8):
        unit[p] = normalize(p)

    pl.semaphore_wait(barrier, len(partners))

    def z_copy(p):
        return pltpu.make_async_remote_copy(
            src_ref=unit.at[p],
            dst_ref=slots.at[0, pl.ds(p * PIECE, PIECE), :],
            send_sem=z_send.at[p],
            recv_sem=z_recv.at[p],
            device_id=plane(-OFFSETS[p]),
            device_id_type=MESH,
        )

    edges = (
        (0, 1, (0, -1), 0), (0, 2, (0, 1), 0), (2, 3, (-1, 0), 0), (2, 4, (1, 0), 0), (3, 5, (-1, 0), 1), (4, 5, (1, 0), 2),
        (0, 6, None, 0), (1, 7, None, 0), (3, 8, None, 0),
    )

    def t_copy(e, n):
        source, target, way, part = edges[e]
        first, amount = STEPS[n][0] * PIECE, STEPS[n][1] * PIECE
        if part:
            amount //= 2
            first += amount * (part - 1)
        where = chip(0, 0, True) if way is None else chip(way[0], way[1], False)
        return pltpu.make_async_remote_copy(
            src_ref=slots.at[source, pl.ds(first, amount), :],
            dst_ref=slots.at[target, pl.ds(first, amount), :],
            send_sem=t_send.at[e, n],
            recv_sem=t_recv.at[e, n],
            device_id=where,
            device_id_type=MESH,
        )

    def prepare():
        def offset_of(slot):
            du, dv = COVER[slot] if slot < 6 else COVER[SIBLING[slot - 6]][::-1]
            nu, nv = (u + du + 4) % 4, (v + dv + 4) % 4
            nx = jnp.where(flip, nv, nu)
            ny = jnp.where(flip, nu, nv)
            nc = c if slot < 6 else 1 - c
            return nx * 512 + ny * 128 + nc * 64

        def steps_before(p):
            return ((z + OFFSETS[p] + 8) % 8) * 2048

        for slot in range(6):
            start = offset_of(slot)
            for p in range(8):
                position = (start + steps_before(p)) + lax.broadcasted_iota(jnp.int32, (PIECE, 128), 0)
                ids = jnp.zeros((PIECE, 128), jnp.int32)
                for m in range(1, 8):
                    ids += jnp.where(position >= bound_ref[m : m + 1, :], 1, 0)
                idr[slot, p * PIECE : (p + 1) * PIECE, :] = ids
        for slot in (0, 2, 3, 4, 5, 6, 7, 8):
            start = offset_of(slot)
            for q in range(4):
                lane = lax.broadcasted_iota(jnp.int32, (8, 128), 1)
                position = jnp.where(lane < 64, start + steps_before(2 * q) + lane, start + steps_before(2 * q + 1) + lane - 64)
                ids = jnp.zeros((8, 128), jnp.int32)
                for m in range(1, 8):
                    ids += jnp.where(position >= bound_ref[m : m + 1, :], 1, 0)
                idc[slot, :, q * 128 : (q + 1) * 128] = ids
        rowacc[...] = jnp.full(rowacc.shape, -1.0, jnp.float32)
        colacc[...] = jnp.full(colacc.shape, -1.0, jnp.float32)

    def quadrant(i, j, a, b, diagonal):
        rows = pl.ds(pl.multiple_of(a * 256, 256), 256)
        cols = pl.ds(pl.multiple_of(b * 256, 256), 256)
        scores = lax.dot_general(
            slots[i, rows, :], slots[j, cols, :], (((1,), (1,)), ((), ())), preferred_element_type=jnp.float32
        )
        best = rowacc[i, rows, :]
        for m in range(2):
            part = scores[:, m * 128 : (m + 1) * 128]
            their = idc[j, 0:1, pl.ds(pl.multiple_of(b * 256 + m * 128, 128), 128)]
            keep = idr[i, rows, :] == their
            if diagonal:
                row = lax.broadcasted_iota(jnp.int32, (256, 128), 0)
                col = lax.broadcasted_iota(jnp.int32, (256, 128), 1) + m * 128
                keep = jnp.logical_and(keep, row != col)
            part = jnp.where(keep, part, -1.0)
            best = jnp.maximum(best, part)
            at = pl.ds(pl.multiple_of(b * 256 + m * 128, 128), 128)
            colacc[j, :, at] = jnp.maximum(colacc[j, :, at], jnp.max(part.reshape(32, 8, 128), axis=0))
        rowacc[i, rows, :] = best

    which = (v // 2, u // 2, c)

    def early():
        def body(n, carry):
            quadrant(pick(n, [a for a, _ in FULL]), pick(n, [b for _, b in FULL]), 0, 0, False)
            return carry

        lax.fori_loop(0, len(FULL), body, 0)
        quadrant(0, 0, 0, 0, True)

    def late():
        def full(n, carry):
            i, j = pick(n, [a for a, _ in FULL]), pick(n, [b for _, b in FULL])
            for a, b in ((0, 1), (1, 0), (1, 1)):
                quadrant(i, j, a, b, False)
            return carry

        def half(n, carry):
            i, j = pick(n, [a for a, _, _ in HALF]), pick(n, [b for _, b, _ in HALF])
            quadrant(i, j, 0, 1, False)
            kind = pick(n, [k for _, _, k in HALF])
            h = jnp.where(kind == 0, which[0], jnp.where(kind == 1, which[1], which[2]))
            quadrant(i, j, h, h, False)
            return carry

        lax.fori_loop(0, len(FULL), full, 0)
        lax.fori_loop(0, len(HALF), half, 0)
        quadrant(0, 0, 0, 1, False)
        quadrant(0, 0, 1, 1, True)

    last = len(STEPS)
    for p in SENT[0]:
        z_copy(p).start()
    for tick in range(last + 3):
        if tick < last:
            first, amount = STEPS[tick]
            for p in range(max(first, 1), first + amount):
                z_copy(p).wait_recv()
            for e in (0, 1, 6):
                t_copy(e, tick).start()
            for p in SENT[tick + 1]:
                z_copy(p).start()
        if tick == 0:
            prepare()
        if 1 <= tick <= last:
            t_copy(1, tick - 1).wait_recv()
            t_copy(2, tick - 1).start()
            t_copy(3, tick - 1).start()
            t_copy(0, tick - 1).wait_recv()
            t_copy(7, tick - 1).start()
        if 2 <= tick <= last + 1:
            t_copy(2, tick - 2).wait_recv()
            t_copy(4, tick - 2).start()
            t_copy(8, tick - 2).start()
            t_copy(3, tick - 2).wait_recv()
            t_copy(5, tick - 2).start()
        if tick >= 3:
            for e in (4, 5, 6, 7, 8):
                t_copy(e, tick - 3).wait_recv()
        if tick == 5:
            early()
    late()

    for slot in range(9):
        best = jnp.max(colacc[slot], axis=0, keepdims=True)
        if slot < 6:
            best = jnp.maximum(best, jnp.max(rowacc[slot].T, axis=0, keepdims=True))
        res[slot] = best

    def r_copy(slot):
        du, dv = COVER[slot] if slot < 6 else COVER[SIBLING[slot - 6]][::-1]
        return pltpu.make_async_remote_copy(
            src_ref=res.at[slot],
            dst_ref=inb.at[slot],
            send_sem=r_send.at[slot],
            recv_sem=r_recv.at[slot],
            device_id=chip(du, dv, slot >= 6),
            device_id_type=MESH,
        )

    for slot in range(1, 9):
        r_copy(slot).start()
    best = res[0]
    for slot in range(1, 9):
        r_copy(slot).wait_recv()
        best = jnp.maximum(best, inb[slot])
    for q in range(4):
        near[q] = best[:, q * 128 : (q + 1) * 128]

    def o_copy(p):
        return pltpu.make_async_remote_copy(
            src_ref=near.at[p // 2],
            dst_ref=obuf.at[p],
            send_sem=o_send.at[p],
            recv_sem=o_recv.at[p],
            device_id=plane(OFFSETS[p]),
            device_id_type=MESH,
        )

    for p in range(1, 8):
        o_copy(p).start()
    out_ref[z] = near[0][:, 0:PIECE]
    for p in range(1, 8):
        o_copy(p).wait_recv()
        k = (z - OFFSETS[p] + 8) % 8
        out_ref[k] = obuf[p][:, (p % 2) * PIECE : (p % 2 + 1) * PIECE]
    for p in range(1, 8):
        z_copy(p).wait_send()
        o_copy(p).wait_send()
    for slot in range(1, 9):
        r_copy(slot).wait_send()
    for e in range(len(edges)):
        for n in range(last):
            t_copy(e, n).wait_send()


def local(embeddings, cluster_ids):
    ids = cluster_ids[0]
    below = jnp.sum(ids[None, :] < jnp.arange(8, dtype=jnp.int32)[:, None], axis=1, dtype=jnp.int32)
    mine = jnp.arange(8, dtype=jnp.int32)[:, None] == lax.axis_index("group")
    table = lax.psum(jnp.where(mine, below[None, :], 0), ("group", "tile"))
    bounds = lax.dynamic_index_in_dim(table, lax.axis_index("tile") // 4, 0, keepdims=False)
    bounds = jnp.broadcast_to(bounds[:, None], (8, 128))
    dma = pltpu.SemaphoreType.DMA
    out = pl.pallas_call(
        kernel,
        out_shape=jax.ShapeDtypeStruct((8, 1, PIECE), jnp.float32),
        in_specs=[pl.BlockSpec(memory_space=pltpu.VMEM)] * 2,
        out_specs=pl.BlockSpec(memory_space=pltpu.VMEM),
        scratch_shapes=[
            pltpu.VMEM((8, PIECE, D), jnp.bfloat16),
            pltpu.VMEM((9, ROWS, D), jnp.bfloat16),
            pltpu.VMEM((6, ROWS, 128), jnp.int32),
            pltpu.VMEM((9, 8, ROWS), jnp.int32),
            pltpu.VMEM((6, ROWS, 128), jnp.float32),
            pltpu.VMEM((9, 8, ROWS), jnp.float32),
            pltpu.VMEM((9, 1, ROWS), jnp.float32),
            pltpu.VMEM((9, 1, ROWS), jnp.float32),
            pltpu.VMEM((4, 1, 128), jnp.float32),
            pltpu.VMEM((8, 1, 128), jnp.float32),
            dma((8,)), dma((8,)), dma((9, 5)), dma((9, 5)), dma((9,)), dma((9,)), dma((8,)), dma((8,)),
        ],
        compiler_params=pltpu.CompilerParams(
            collective_id=0, has_side_effects=True, vmem_limit_bytes=40 * 1024 * 1024
        ),
        cost_estimate=pl.CostEstimate(flops=2 * 17 * 512 * 512 * 768, bytes_accessed=1 << 20, transcendentals=0),
    )(embeddings, bounds)
    return out.reshape(1, ROWS)


def solution(mesh):
    in_specs = (P("group", "tile", None), P("group", "tile"))
    out_specs = P("group", "tile")
    return jax.shard_map(local, mesh=mesh, in_specs=in_specs, out_specs=out_specs, check_vma=False)
```

time: 336 us -> 146 us (0.43)
  waiting for transfers between devices: 135 us -> 0 us
  matrix products: 64.7 us -> 0 us
  Pallas kernels: 0 us -> 63.4 us
  other arithmetic: 22.7 us -> 0.86 us
  local copies, waits for them, and re-layouts: 20.2 us -> 3.05 us
  between operations: 13.5 us -> 0.02 us
    all_gather x1 -> x0, waiting for transfers between devices: 135 us -> none  [local(): piece = lax.all_gather(routed, 'tile', axis=0, tiled=True)]
    psum x0 -> x1, blocking collectives: none -> 78.4 us  [local(): table = lax.psum(jnp.where(mine, below[None, :], 0), ('group', 'tile'))]
    dot_general x32 -> x0, matrix products: 64.7 us -> none  [scored(): jnp.einsum('rd,cd->rc', routed, piece, preferred_element_type=jnp.float32)]
    pallas_call x0 -> x1, Pallas kernels: none -> 63.4 us  [local(): pl.pallas_call(kernel, out_shape=jax.ShapeDtypeStruct((8, 1, PIECE), jnp....]
    all_gather x1 -> x0, blocking collectives: 51.4 us -> none  [local(): piece_ids = lax.all_gather(wire_ids, 'tile', axis=0, tiled=True)]
    all_to_all x2 -> x0, blocking collectives: 24 us -> none  [the longest x1 16.2 us: local(): lax.all_to_all(unit.reshape(groups, portion, width), 'group', split_axis=...]
    dynamic_slice x32 -> x0, local copies, waits for them, and re-layouts: 18.8 us -> none  [local(): result, _ = lax.scan(visit, start_best, items)]
    add x32 -> x0, other arithmetic: 18.3 us -> none  [local(): own_index = mine * length + jnp.arange(length, dtype=jnp.int32)]
  transfers between devices with their start and end apart: 1 -> 0, of which waited for: 1 -> 0; matrix products, arithmetic and copies ran while one was open for 0% -> 0% of each run, Pallas kernels for 0% -> 0%
where the time goes in v1:
time: 146 us
  blocking collectives  78.4 us (54%)
  Pallas kernels  63.4 us (43%)
  local copies, waits for them, and re-layouts  3.05 us (2%)
    psum x1, blocking collectives, local(): table = lax.psum(jnp.where(mine, below[None, :], 0), ('group', 'tile'))  78.4 us
    pallas_call x1, Pallas kernels, local(): pl.pallas_call(kernel, out_shape=jax.ShapeDtypeStruct((8, 1, PIECE), jnp....  63.4 us

profile of v1, /device:TPU:24, one launch (start us, length us, event | category | flops | bytes accessed | tf_op | source)
XLA Modules:
  0.0 145.7 jit_solution(11864562336220685868)
XLA Ops:
  0.0 0.0 copy-start.1
  0.0 0.7 copy-done.1
  0.7 0.1 convert_reduce_fusion
  0.8 0.1 broadcast_select_fusion
  0.9 78.4 %psum.7 = s32[8,8]{1,0:T(8,128)S(1)} all-reduce(s32[8,8]{1,0:T(8,128)S(1)} %broadcast_select_fusion), channel_id=1, replica_groups=mesh['group'=8,'tile'=32] {'group','tile'}, use_global_device_ids=true, to_apply=%region_1.2 | all-reduce | flops 64 | bytes 512 | tf_op jit(solution)/shard_map/psum | solution.py:277
  79.2 0.1 broadcast_in_dim.35.bound_ref
  79.3 0.0 copy-start
  79.3 1.1 copy-done
  80.4 63.4 %shard_map.28 = f32[8,1,64]{2,1,0:T(1,128)S(1)} custom-call(bf16[1,512,768]{2,1,0:T(8,128)(2,1)S(1)} %copy-done, s32[8,128]{1,0:T(8,128)S(1)} %broadcast_in_dim.35.bound_ref), custom_call_target="tpu_custom_call" | custom-call | flops 6845104128 | bytes 1048576 | tf_op jit(solution)/shard_map/pallas_call | solution.py:281
  143.9 0.5 broadcast.10
  144.4 0.7 reduce.3
  145.1 0.7 reshape.11
  (2 shorter events, 0.0 us)
Async XLA Ops:
  0.0 0.7 copy-start.1
  79.3 1.1 copy-start

commit v2 on v0

v2 whole, which is shorter than its diff:
```python
import functools

import jax
import jax.numpy as jnp
from jax import lax
from jax.experimental import pallas as pl
from jax.experimental.pallas import tpu as pltpu
from jax.sharding import PartitionSpec as P

MESH = pl.DeviceIdType.MESH
D = 768
ROWS = 512
PIECE = 64

COVER = ((0, 0), (0, 1), (0, -1), (1, -1), (-1, -1), (2, -1))
SIBLING = (0, 1, 3)
OFFSETS = (0, 1, -1, 2, -2, 3, -3, 4)
FULL = ((0, 2), (0, 3), (0, 4), (2, 3), (2, 6), (4, 6), (4, 8), (1, 6), (0, 5), (5, 6), (5, 8))
HALF_FIRST = ((0, 6, 2), (3, 6, 2), (3, 8, 2))
HALF_LAST = ((1, 2, 0), (1, 3, 0), (1, 4, 0), (1, 7, 2), (1, 5, 0), (2, 5, 1))
EDGES = (
    (0, 1, (0, -1)), (0, 2, (0, 1)), (2, 3, (-1, 0)), (2, 4, (1, 0)), (3, 5, (-1, 0)), (4, 5, (1, 0)),
    (0, 6, None), (1, 7, None), (3, 8, None), (2, 0, (0, -1)), (2, 5, (2, 0)),
)
LAST = 7
DIRECT = 5


def pick(n, table):
    value = jnp.int32(table[0])
    for at in range(1, len(table)):
        value = jnp.where(n == at, jnp.int32(table[at]), value)
    return value


def kernel(
    x_ref, id_ref, out_ref,
    raw, unit, slots, idr, idc, rowacc, colacc, res, inb, near, obuf, count, total, spread, bound,
    x_sem, z_send, z_recv, t_send, t_recv, r_send, r_recv, o_send, o_recv,
    a_send, a_recv, b_send, b_recv, c_send, c_recv,
):
    group = lax.axis_index("group")
    tile = lax.axis_index("tile")
    y, c = group // 2, group % 2
    z, x = tile // 4, tile % 4
    flip = c == 1
    u = jnp.where(flip, y, x)
    v = jnp.where(flip, x, y)

    def place(du, dv):
        nu, nv = (u + du + 4) % 4, (v + dv + 4) % 4
        return jnp.where(flip, nv, nu), jnp.where(flip, nu, nv)

    def chip(du, dv, other, dz=0):
        nx, ny = place(du, dv)
        nc = 1 - c if other else c
        return {"group": ny * 2 + nc, "tile": ((z + dz + 8) % 8) * 4 + nx}

    def plane(dz):
        return {"group": group, "tile": ((z + dz + 8) % 8) * 4 + x}

    def input_copy(p):
        k = (z - OFFSETS[p] + 8) % 8
        rows = pl.ds(pl.multiple_of(k * PIECE, PIECE), PIECE)
        return pltpu.make_async_copy(x_ref.at[0, rows, :], raw.at[p], x_sem.at[p])

    for p in range(8):
        input_copy(p).start()

    barrier = pltpu.get_barrier_semaphore()
    partners = [plane(o) for o in range(1, 8)]
    partners += [chip(a, b, False) for a, b in ((0, 1), (0, -1), (1, 0), (-1, 0), (1, -1), (-1, 1), (-1, -1), (1, 1), (2, -1), (2, 1), (0, 2), (2, 0))]
    partners += [chip(a, b, True) for a, b in ((0, 0), (1, 0), (0, -1), (-1, 1))]
    partners += [chip(jnp.where(flip, -1, 0), jnp.where(flip, 0, 1), True), chip(jnp.where(flip, 2, 0), jnp.where(flip, 0, 2), True)]
    partners += [chip(0, 1, False, 4), chip(0, -1, False, 4)]
    for partner in partners:
        pl.semaphore_signal(barrier, inc=1, device_id=partner, device_id_type=MESH)

    def normalize(p):
        input_copy(p).wait()
        values = raw[p].astype(jnp.float32)
        size = jnp.sum(values * values, axis=1, keepdims=True) + 1e-06
        return (values * (1.0 / jnp.sqrt(size))).astype(jnp.bfloat16)

    slots[0, 0:PIECE, :] = normalize(0)
    for p in range(1, 8):
        unit[p] = normalize(p)
    for m in range(8):
        below = jnp.zeros((1, 128), jnp.float32)
        for q in range(4):
            below += jnp.where(id_ref[:, q * 128 : (q + 1) * 128] < m, 1.0, 0.0)
        count[z, m : m + 1, :] = below

    pl.semaphore_wait(barrier, len(partners))

    def z_copy(p):
        return pltpu.make_async_remote_copy(
            src_ref=unit.at[p],
            dst_ref=slots.at[2 if p == LAST else 0, pl.ds(p * PIECE, PIECE), :],
            send_sem=z_send.at[p],
            recv_sem=z_recv.at[p],
            device_id=chip(0, 1, False, -OFFSETS[p]) if p == LAST else plane(-OFFSETS[p]),
            device_id_type=MESH,
        )

    def t_copy(e, p):
        source, target, way = EDGES[e]
        first, amount = p * PIECE, PIECE
        return pltpu.make_async_remote_copy(
            src_ref=slots.at[source, pl.ds(first, amount), :],
            dst_ref=slots.at[target, pl.ds(first, amount), :],
            send_sem=t_send.at[e, p],
            recv_sem=t_recv.at[e, p],
            device_id=chip(0, 0, True) if way is None else chip(way[0], way[1], False),
            device_id_type=MESH,
        )

    def edges_of(p):
        if p == LAST:
            return (0, 2, 3, 6, 7, 8, 9, 10)
        return (0, 1, 2, 3, 10 if p >= DIRECT else 4 + p % 2, 6, 7, 8)

    def go(p, *edges):
        for e in edges:
            if e in edges_of(p):
                t_copy(e, p).start()

    def come(p, *edges):
        for e in edges:
            if e in edges_of(p):
                t_copy(e, p).wait_recv()

    def root(*pieces):
        for p in pieces:
            if p:
                z_copy(p).wait_recv()
            go(p, 0, 1, 6)

    def second(*pieces):
        for p in pieces:
            come(p, 1)
            go(p, 2, 3, 10)
            come(p, 0)
            go(p, 7)

    def third(*pieces):
        for p in pieces:
            come(p, 2)
            go(p, 4, 8)
            come(p, 3)
            go(p, 5)

    holder = group == z

    def a_copy(sender):
        return pltpu.make_async_remote_copy(
            src_ref=count.at[sender], dst_ref=count.at[sender], send_sem=a_send, recv_sem=a_recv.at[sender],
            device_id={"group": group, "tile": group * 4 + x}, device_id_type=MESH,
        )

    def b_copy(n):
        return pltpu.make_async_remote_copy(
            src_ref=total, dst_ref=spread.at[0], send_sem=b_send.at[n], recv_sem=b_recv,
            device_id={"group": (group + n) % 8, "tile": tile}, device_id_type=MESH,
        )

    def c_copy(n):
        return pltpu.make_async_remote_copy(
            src_ref=spread.at[0], dst_ref=spread.at[n], send_sem=c_send.at[n], recv_sem=c_recv.at[n],
            device_id={"group": group, "tile": z * 4 + (x + n) % 4}, device_id_type=MESH,
        )

    def bounds_a():
        @pl.when(jnp.logical_not(holder))
        def _():
            a_copy(z).start()

    def bounds_b():
        @pl.when(holder)
        def _():
            for n in range(1, 8):
                a_copy((z + n) % 8).wait_recv()
            value = count[0]
            for n in range(1, 8):
                value += count[n]
            total[...] = value
            spread[0] = value
            for n in range(1, 8):
                b_copy(n).start()

    def bounds_c():
        @pl.when(jnp.logical_not(holder))
        def _():
            b_copy(1).wait_recv()

        for n in range(1, 4):
            c_copy(n).start()

    def bounds_d():
        value = spread[0]
        for n in range(1, 4):
            c_copy(n).wait_recv()
            value += spread[n]
        bound[...] = jnp.broadcast_to(jnp.sum(value, axis=1, keepdims=True), (8, 128)).astype(jnp.int32)

    def bounds_end():
        @pl.when(jnp.logical_not(holder))
        def _():
            a_copy(z).wait_send()

        @pl.when(holder)
        def _():
            for n in range(1, 8):
                b_copy(n).wait_send()

        for n in range(1, 4):
            c_copy(n).wait_send()

    def identify():
        def offset_of(slot):
            nx, ny = place(*(COVER[slot] if slot < 6 else COVER[SIBLING[slot - 6]][::-1]))
            return nx * 512 + ny * 128 + (c if slot < 6 else 1 - c) * 64

        def steps_before(p):
            return ((z + OFFSETS[p] + 8) % 8) * 2048

        def cluster(position):
            ids = jnp.zeros(position.shape, jnp.int32)
            for m in range(1, 8):
                ids += jnp.where(position >= bound[m : m + 1, :], 1, 0)
            return ids

        for slot in range(6):
            start = offset_of(slot)
            for p in range(8):
                position = (start + steps_before(p)) + lax.broadcasted_iota(jnp.int32, (PIECE, 128), 0)
                idr[slot, p * PIECE : (p + 1) * PIECE, :] = cluster(position)
        for slot in (0, 2, 3, 4, 5, 6, 7, 8):
            start = offset_of(slot)
            for q in range(4):
                lane = lax.broadcasted_iota(jnp.int32, (8, 128), 1)
                position = jnp.where(lane < 64, start + steps_before(2 * q) + lane, start + steps_before(2 * q + 1) + lane - 64)
                idc[slot, :, q * 128 : (q + 1) * 128] = cluster(position)

    def clear():
        rowacc[...] = jnp.full(rowacc.shape, -1.0, jnp.float32)
        colacc[...] = jnp.full(colacc.shape, -1.0, jnp.float32)

    def score(i, j, rows, cols, diagonal=False):
        height = rows[1]
        rows = pl.ds(rows[0], height)
        scores = lax.dot_general(
            slots[i, rows, :], slots[j, pl.ds(cols[0], cols[1]), :], (((1,), (1,)), ((), ())),
            preferred_element_type=jnp.float32,
        )
        best = rowacc[i, rows, :]
        for m in range(cols[1] // 128):
            part = scores[:, m * 128 : (m + 1) * 128]
            at = cols[0] + m * 128
            at = pl.ds(at if isinstance(at, int) else pl.multiple_of(at, 128), 128)
            keep = idr[i, rows, :] == idc[j, 0:1, at]
            if diagonal:
                row = lax.broadcasted_iota(jnp.int32, (height, 128), 0)
                col = lax.broadcasted_iota(jnp.int32, (height, 128), 1) + m * 128
                keep = jnp.logical_and(keep, row != col)
            part = jnp.where(keep, part, -1.0)
            best = jnp.maximum(best, part)
            colacc[j, :, at] = jnp.maximum(colacc[j, :, at], jnp.max(part.reshape(height // 8, 8, 128), axis=0))
        rowacc[i, rows, :] = best

    def loop(table, body, together):
        def step(n, carry):
            for at in range(together):
                body([pick(n, column) for column in zip(*table[at::together])])
            return carry

        if len(table) == together:
            for entry in table:
                body(entry)
        else:
            lax.fori_loop(0, len(table) // together, step, 0)

    def early(entry):
        score(entry[0], entry[1], (0, 256), (0, 256))

    def late(entry):
        score(entry[0], entry[1], (0, 512), (256, 256))
        score(entry[0], entry[1], (256, 256), (0, 256))

    def half(entry):
        i, j, kind = entry
        h = jnp.where(kind == 0, v // 2, jnp.where(kind == 1, u // 2, c))
        h = pl.multiple_of(h * 256, 256)
        score(i, j, (0, 256), (256, 256))
        score(i, j, (h, 256), (h, 256))

    def settle(slot):
        best = jnp.max(colacc[slot], axis=0, keepdims=True) if slot != 1 else None
        if slot < 6:
            rows = jnp.max(rowacc[slot].T, axis=0, keepdims=True)
            best = rows if best is None else jnp.maximum(best, rows)
        res[slot] = best

    def r_copy(slot):
        du, dv = COVER[slot] if slot < 6 else COVER[SIBLING[slot - 6]][::-1]
        return pltpu.make_async_remote_copy(
            src_ref=res.at[slot], dst_ref=inb.at[slot], send_sem=r_send.at[slot], recv_sem=r_recv.at[slot],
            device_id=chip(du, dv, slot >= 6), device_id_type=MESH,
        )

    def answer(*chosen):
        for slot in chosen:
            settle(slot)
            r_copy(slot).start()

    z_copy(1).start()
    z_copy(2).start()
    root(0)
    z_copy(3).start()
    z_copy(4).start()
    bounds_a()
    clear()
    second(0)
    root(1, 2)
    z_copy(5).start()
    z_copy(6).start()
    third(0)
    bounds_b()
    second(1, 2)
    root(3, 4)
    z_copy(LAST).start()
    third(1, 2)
    bounds_c()
    second(3, 4)
    bounds_d()
    identify()
    root(5, 6)
    third(3, 4)
    for p in range(4):
        come(p, 6, 7, 8)
    loop(FULL[:8], early, 4)
    second(5, 6)
    z_copy(LAST).wait_recv()
    go(LAST, 2, 3, 9, 10)
    for p in range(4):
        come(p, 4, 5)
    loop(FULL[8:], early, 3)
    score(0, 0, (0, 256), (0, 256), True)
    third(5, 6)
    come(LAST, 9)
    go(LAST, 0, 6)
    third(LAST)
    loop(FULL[:4], late, 4)
    score(0, 0, (0, 256), (256, 256))
    score(0, 0, (256, 256), (256, 256), True)
    for p in range(4, 7):
        come(p, 6, 8)
    come(LAST, 6, 8)
    loop(FULL[4:7], late, 3)
    loop(HALF_FIRST, half, 3)
    come(LAST, 0)
    go(LAST, 7)
    loop(FULL[7:8], late, 1)
    loop(HALF_LAST[:3], half, 3)
    answer(3, 4)
    for p in range(4, 8):
        come(p, 7)
    loop(HALF_LAST[3:4], half, 1)
    answer(7)
    for p in range(4, 8):
        come(p, 4, 5, 10)
    loop(FULL[8:], late, 3)
    loop(HALF_LAST[4:], half, 2)
    answer(5, 1, 2, 6, 8)
    settle(0)
    bounds_end()
    for p in range(8):
        if p:
            z_copy(p).wait_send()
        for e in edges_of(p):
            t_copy(e, p).wait_send()

    best = res[0]
    for slot in (3, 4, 7, 5, 1, 2, 6, 8):
        r_copy(slot).wait_recv()
        best = jnp.maximum(best, inb[slot])
    lane = lax.broadcasted_iota(jnp.int32, (1, 128), 1)
    for p in range(8):
        part = best[:, p // 2 * 128 : (p // 2 + 1) * 128]
        turned = pltpu.roll(part, 64, 1)
        near[p] = jnp.where((lane < 64) == (p % 2 == 0), part, turned)

    def o_copy(p):
        return pltpu.make_async_remote_copy(
            src_ref=near.at[p], dst_ref=obuf.at[z], send_sem=o_send.at[p], recv_sem=o_recv.at[p],
            device_id=plane(OFFSETS[p]), device_id_type=MESH,
        )

    for p in (7, 5, 6, 3, 4, 1, 2):
        o_copy(p).start()
    obuf[z] = near[0]
    for slot in range(1, 9):
        r_copy(slot).wait_send()
    for p in (1, 2, 3, 4, 5, 6, 7):
        o_copy(p).wait_recv()
    for q in range(4):
        out_ref[:, q * 128 : (q + 1) * 128] = jnp.where(lane < 64, obuf[2 * q], obuf[2 * q + 1])
    for p in range(1, 8):
        o_copy(p).wait_send()


def local(embeddings, cluster_ids):
    dma = pltpu.SemaphoreType.DMA
    return pl.pallas_call(
        kernel,
        out_shape=jax.ShapeDtypeStruct((1, ROWS), jnp.float32),
        in_specs=[pl.BlockSpec(memory_space=pl.ANY), pl.BlockSpec(memory_space=pltpu.VMEM)],
        out_specs=pl.BlockSpec(memory_space=pltpu.VMEM),
        scratch_shapes=[
            pltpu.VMEM((8, PIECE, D), jnp.bfloat16),
            pltpu.VMEM((8, PIECE, D), jnp.bfloat16),
            pltpu.VMEM((9, ROWS, D), jnp.bfloat16),
            pltpu.VMEM((6, ROWS, 128), jnp.int32),
            pltpu.VMEM((9, 8, ROWS), jnp.int32),
            pltpu.VMEM((6, ROWS, 128), jnp.float32),
            pltpu.VMEM((9, 8, ROWS), jnp.float32),
            pltpu.VMEM((9, 1, ROWS), jnp.float32),
            pltpu.VMEM((9, 1, ROWS), jnp.float32),
            pltpu.VMEM((8, 1, 128), jnp.float32),
            pltpu.VMEM((8, 1, 128), jnp.float32),
            pltpu.VMEM((8, 8, 128), jnp.float32),
            pltpu.VMEM((8, 128), jnp.float32),
            pltpu.VMEM((4, 8, 128), jnp.float32),
            pltpu.VMEM((8, 128), jnp.int32),
            dma((8,)), dma((8,)), dma((8,)), dma((11, 8)), dma((11, 8)), dma((9,)), dma((9,)), dma((8,)), dma((8,)),
            dma, dma((8,)), dma((8,)), dma, dma((4,)), dma((4,)),
        ],
        compiler_params=pltpu.CompilerParams(
            collective_id=0, has_side_effects=True, vmem_limit_bytes=40 * 1024 * 1024
        ),
        cost_estimate=pl.CostEstimate(flops=2 * 17 * 512 * 512 * 768, bytes_accessed=1 << 20, transcendentals=0),
    )(embeddings, cluster_ids)


def solution(mesh):
    in_specs = (P("group", "tile", None), P("group", "tile"))
    out_specs = P("group", "tile")
    return jax.shard_map(local, mesh=mesh, in_specs=in_specs, out_specs=out_specs, check_vma=False)
```

time: 336 us -> 69.5 us (0.21); the launches traced: 332 us -> 69.3 us
  waiting for transfers between devices: 135 us -> 0 us
  blocking collectives: 75.4 us -> 0 us
  Pallas kernels: 0 us -> 66.9 us
  matrix products: 64.7 us -> 0 us
  other arithmetic: 22.7 us -> 0 us
  local copies, waits for them, and re-layouts: 20.2 us -> 2.39 us
  between operations: 13.5 us -> 0.01 us
    all_gather x1 -> x0, waiting for transfers between devices: 135 us -> none  [local(): piece = lax.all_gather(routed, 'tile', axis=0, tiled=True)]
    pallas_call x0 -> x1, Pallas kernels: none -> 66.9 us  [local(): pl.pallas_call(kernel, out_shape=jax.ShapeDtypeStruct((1, ROWS), jnp.floa...]
    dot_general x32 -> x0, matrix products: 64.7 us -> none  [scored(): jnp.einsum('rd,cd->rc', routed, piece, preferred_element_type=jnp.float32)]
    all_gather x1 -> x0, blocking collectives: 51.4 us -> none  [local(): piece_ids = lax.all_gather(wire_ids, 'tile', axis=0, tiled=True)]
    all_to_all x2 -> x0, blocking collectives: 24 us -> none  [the longest x1 16.2 us: local(): lax.all_to_all(unit.reshape(groups, portion, width), 'group', split_axis=...]
    dynamic_slice x32 -> x0, local copies, waits for them, and re-layouts: 18.8 us -> none  [local(): result, _ = lax.scan(visit, start_best, items)]
    add x32 -> x0, other arithmetic: 18.3 us -> none  [local(): own_index = mine * length + jnp.arange(length, dtype=jnp.int32)]
  transfers between devices with their start and end apart: 1 -> 0, of which waited for: 1 -> 0; matrix products, arithmetic and copies ran while one was open for 0% -> 0% of each run, Pallas kernels for 0% -> 0%
where the time goes in v2:
time: 69.5 us; the launch traced here: 69.3 us
  Pallas kernels  66.9 us (96%)
  local copies, waits for them, and re-layouts  2.39 us (3%)
    pallas_call x1, Pallas kernels, local(): pl.pallas_call(kernel, out_shape=jax.ShapeDtypeStruct((1, ROWS), jnp.floa...  66.9 us
    unnamed x5, local copies, waits for them, and re-layouts  2.39 us

profile of v2, /device:TPU:24, one launch (start us, length us, event | category | flops | bytes accessed | tf_op | source)
XLA Modules:
  0.0 69.3 jit_solution(8012829886347386663)
XLA Ops:
  0.0 0.0 copy-start
  0.0 1.1 %copy-done = bf16[1,512,768]{2,1,0:T(8,128)(2,1)S(1)} copy-done((bf16[1,512,768]{2,1,0:T(8,128)(2,1)S(1)}, bf16[1,512,768]{2,1,0:T(8,128)(2,1)}, u32[]{:S(2)}) %copy-start) | copy-done | bytes 786456
  1.1 0.0 copy-start.1
  1.1 0.7 copy-done.1
  1.8 66.9 %shard_map.28 = f32[1,512]{1,0:T(1,128)S(1)} custom-call(bf16[1,512,768]{2,1,0:T(8,128)(2,1)S(1)} %copy-done, s32[1,512]{1,0:T(1,128)S(1)} %copy-done.1), custom_call_target="tpu_custom_call" | custom-call | flops 6845104128 | bytes 1048576 | tf_op jit(solution)/shard_map/pallas_call | solution.py:414
  68.8 0.6 copy.4
Async XLA Ops:
  0.0 1.1 %copy-start = (bf16[1,512,768]{2,1,0:T(8,128)(2,1)S(1)}, bf16[1,512,768]{2,1,0:T(8,128)(2,1)}, u32[]{:S(2)}) copy-start(bf16[1,512,768]{2,1,0:T(8,128)(2,1)} %x_ref.1) | copy-start | bytes 2359300
  1.1 0.7 copy-start.1

commit v3 on v2

--- a/solution.py
+++ b/solution.py
@@ -15,15 +15,13 @@
 COVER = ((0, 0), (0, 1), (0, -1), (1, -1), (-1, -1), (2, -1))
 SIBLING = (0, 1, 3)
 OFFSETS = (0, 1, -1, 2, -2, 3, -3, 4)
-FULL = ((0, 2), (0, 3), (0, 4), (2, 3), (2, 6), (4, 6), (4, 8), (1, 6), (0, 5), (5, 6), (5, 8))
-HALF_FIRST = ((0, 6, 2), (3, 6, 2), (3, 8, 2))
-HALF_LAST = ((1, 2, 0), (1, 3, 0), (1, 4, 0), (1, 7, 2), (1, 5, 0), (2, 5, 1))
+FULL = ((0, 2), (0, 3), (0, 4), (2, 3), (2, 6), (1, 6), (4, 6), (4, 8), (0, 5), (5, 6), (5, 8))
+HALF = ((1, 2, 0), (1, 3, 0), (1, 4, 0), (0, 6, 2), (3, 6, 2), (3, 8, 2), (1, 7, 2), (1, 5, 0), (2, 5, 1))
 EDGES = (
     (0, 1, (0, -1)), (0, 2, (0, 1)), (2, 3, (-1, 0)), (2, 4, (1, 0)), (3, 5, (-1, 0)), (4, 5, (1, 0)),
-    (0, 6, None), (1, 7, None), (3, 8, None), (2, 0, (0, -1)), (2, 5, (2, 0)),
+    (0, 6, None), (1, 7, None), (3, 8, None), (2, 5, (2, 0)),
 )
-LAST = 7
-DIRECT = 5
+DIRECT = 7
 
 
 def pick(n, table):
@@ -72,7 +70,6 @@
     partners += [chip(a, b, False) for a, b in ((0, 1), (0, -1), (1, 0), (-1, 0), (1, -1), (-1, 1), (-1, -1), (1, 1), (2, -1), (2, 1), (0, 2), (2, 0))]
     partners += [chip(a, b, True) for a, b in ((0, 0), (1, 0), (0, -1), (-1, 1))]
     partners += [chip(jnp.where(flip, -1, 0), jnp.where(flip, 0, 1), True), chip(jnp.where(flip, 2, 0), jnp.where(flip, 0, 2), True)]
-    partners += [chip(0, 1, False, 4), chip(0, -1, False, 4)]
     for partner in partners:
         pl.semaphore_signal(barrier, inc=1, device_id=partner, device_id_type=MESH)
 
@@ -96,10 +93,10 @@
     def z_copy(p):
         return pltpu.make_async_remote_copy(
             src_ref=unit.at[p],
-            dst_ref=slots.at[2 if p == LAST else 0, pl.ds(p * PIECE, PIECE), :],
+            dst_ref=slots.at[0, pl.ds(p * PIECE, PIECE), :],
             send_sem=z_send.at[p],
             recv_sem=z_recv.at[p],
-            device_id=chip(0, 1, False, -OFFSETS[p]) if p == LAST else plane(-OFFSETS[p]),
+            device_id=plane(-OFFSETS[p]),
             device_id_type=MESH,
         )
 
@@ -116,9 +113,7 @@
         )
 
     def edges_of(p):
-        if p == LAST:
-            return (0, 2, 3, 6, 7, 8, 9, 10)
-        return (0, 1, 2, 3, 10 if p >= DIRECT else 4 + p % 2, 6, 7, 8)
+        return (0, 1, 2, 3, 9 if p >= DIRECT else 4 + p % 2, 6, 7, 8)
 
     def go(p, *edges):
         for e in edges:
@@ -130,25 +125,26 @@
             if e in edges_of(p):
                 t_copy(e, p).wait_recv()
 
-    def root(*pieces):
-        for p in pieces:
-            if p:
-                z_copy(p).wait_recv()
-            go(p, 0, 1, 6)
-
-    def second(*pieces):
-        for p in pieces:
-            come(p, 1)
-            go(p, 2, 3, 10)
-            come(p, 0)
-            go(p, 7)
-
-    def third(*pieces):
-        for p in pieces:
-            come(p, 2)
-            go(p, 4, 8)
-            come(p, 3)
-            go(p, 5)
+    def root(p):
+        if p:
+            z_copy(p).wait_recv()
+        go(p, 1, 0, 6)
+
+    def into2(p):
+        come(p, 1)
+        go(p, 2, 3, 9)
+
+    def into1(p):
+        come(p, 0)
+        go(p, 7)
+
+    def into3(p):
+        come(p, 2)
+        go(p, 4, 8)
+
+    def into4(p):
+        come(p, 3)
+        go(p, 5)
 
     holder = group == z
 
@@ -216,7 +212,7 @@
         for n in range(1, 4):
             c_copy(n).wait_send()
 
-    def identify():
+    def identify(rows, cols):
         def offset_of(slot):
             nx, ny = place(*(COVER[slot] if slot < 6 else COVER[SIBLING[slot - 6]][::-1]))
             return nx * 512 + ny * 128 + (c if slot < 6 else 1 - c) * 64
@@ -230,12 +226,12 @@
                 ids += jnp.where(position >= bound[m : m + 1, :], 1, 0)
             return ids
 
-        for slot in range(6):
+        for slot in rows:
             start = offset_of(slot)
             for p in range(8):
                 position = (start + steps_before(p)) + lax.broadcasted_iota(jnp.int32, (PIECE, 128), 0)
                 idr[slot, p * PIECE : (p + 1) * PIECE, :] = cluster(position)
-        for slot in (0, 2, 3, 4, 5, 6, 7, 8):
+        for slot in cols:
             start = offset_of(slot)
             for q in range(4):
                 lane = lax.broadcasted_iota(jnp.int32, (8, 128), 1)
@@ -313,64 +309,90 @@
             settle(slot)
             r_copy(slot).start()
 
-    z_copy(1).start()
-    z_copy(2).start()
+    bounds_a()
+    for p in range(1, 3):
+        z_copy(p).start()
     root(0)
-    z_copy(3).start()
-    z_copy(4).start()
-    bounds_a()
+    for p in range(3, 8):
+        z_copy(p).start()
     clear()
-    second(0)
-    root(1, 2)
-    z_copy(5).start()
-    z_copy(6).start()
-    third(0)
+    root(1)
+    root(2)
     bounds_b()
-    second(1, 2)
-    root(3, 4)
-    z_copy(LAST).start()
-    third(1, 2)
+    into2(0)
+    into1(0)
+    root(3)
+    into2(1)
+    into1(1)
+    root(4)
+    into2(2)
+    into1(2)
+    into3(0)
+    into4(0)
+    root(5)
+    into2(3)
+    into1(3)
     bounds_c()
-    second(3, 4)
+    into3(1)
+    into4(1)
+    root(6)
+    into2(4)
+    into1(4)
+    into3(2)
+    into4(2)
+    root(7)
+    into2(5)
+    into4(3)
+    into3(3)
     bounds_d()
-    identify()
-    root(5, 6)
-    third(3, 4)
-    for p in range(4):
-        come(p, 6, 7, 8)
-    loop(FULL[:8], early, 4)
-    second(5, 6)
-    z_copy(LAST).wait_recv()
-    go(LAST, 2, 3, 9, 10)
+    identify((0, 1, 2), ())
+    into2(6)
+    into1(5)
+    into3(4)
+    into4(4)
+    identify((3, 4, 5), ())
+    identify((), (0, 2, 3, 4, 5, 6, 7, 8))
+    into2(7)
+    into4(5)
+    loop(FULL[:4], early, 4)
+    into1(7)
+    loop(FULL[:1], late, 1)
+    into1(6)
+    into3(6)
+    into3(5)
     for p in range(4):
         come(p, 4, 5)
-    loop(FULL[8:], early, 3)
+    loop(FULL[8:9], early, 1)
     score(0, 0, (0, 256), (0, 256), True)
-    third(5, 6)
-    come(LAST, 9)
-    go(LAST, 0, 6)
-    third(LAST)
-    loop(FULL[:4], late, 4)
+    into4(6)
+    for p in range(4):
+        come(p, 6, 8)
+    loop(FULL[4:8], early, 4)
+    loop(FULL[9:], early, 2)
+    for p in range(4, 8):
+        come(p, 6)
+    loop(FULL[4:6], late, 2)
+    loop(HALF[3:4], half, 1)
+    into4(7)
+    loop(HALF[:1], half, 1)
     score(0, 0, (0, 256), (256, 256))
     score(0, 0, (256, 256), (256, 256), True)
-    for p in range(4, 7):
-        come(p, 6, 8)
-    come(LAST, 6, 8)
-    loop(FULL[4:7], late, 3)
-    loop(HALF_FIRST, half, 3)
-    come(LAST, 0)
-    go(LAST, 7)
+    into3(7)
+    loop(FULL[1:4], late, 3)
+    loop(FULL[6:7], late, 1)
+    loop(HALF[1:3], half, 2)
+    loop(HALF[4:5], half, 1)
+    for p in range(4, 8):
+        come(p, 8)
     loop(FULL[7:8], late, 1)
-    loop(HALF_LAST[:3], half, 3)
-    answer(3, 4)
+    for p in range(8):
+        come(p, 7)
+    loop(HALF[5:7], half, 2)
+    answer(3, 4, 7)
     for p in range(4, 8):
-        come(p, 7)
-    loop(HALF_LAST[3:4], half, 1)
-    answer(7)
-    for p in range(4, 8):
-        come(p, 4, 5, 10)
+        come(p, 4, 5, 9)
     loop(FULL[8:], late, 3)
-    loop(HALF_LAST[4:], half, 2)
+    loop(HALF[7:], half, 2)
     answer(5, 1, 2, 6, 8)
     settle(0)
     bounds_end()
@@ -432,7 +454,7 @@
             pltpu.VMEM((8, 128), jnp.float32),
             pltpu.VMEM((4, 8, 128), jnp.float32),
             pltpu.VMEM((8, 128), jnp.int32),
-            dma((8,)), dma((8,)), dma((8,)), dma((11, 8)), dma((11, 8)), dma((9,)), dma((9,)), dma((8,)), dma((8,)),
+            dma((8,)), dma((8,)), dma((8,)), dma((10, 8)), dma((10, 8)), dma((9,)), dma((9,)), dma((8,)), dma((8,)),
             dma, dma((8,)), dma((8,)), dma, dma((4,)), dma((4,)),
         ],
         compiler_params=pltpu.CompilerParams(

time: 69.5 us -> 62 us (0.89)
  Pallas kernels: 66.9 us -> 59.4 us
    pallas_call x1, Pallas kernels: 66.9 us -> 59.4 us  [local(): pl.pallas_call(kernel, out_shape=jax.ShapeDtypeStruct((1, ROWS), jnp.floa...]
where the time goes in v3:
time: 62 us; the launch traced here: 61.8 us
  Pallas kernels  59.4 us (96%)
  local copies, waits for them, and re-layouts  2.39 us (4%)
    pallas_call x1, Pallas kernels, local(): pl.pallas_call(kernel, out_shape=jax.ShapeDtypeStruct((1, ROWS), jnp.floa...  59.4 us
    unnamed x5, local copies, waits for them, and re-layouts  2.39 us

profile of v3, /device:TPU:24, one launch (start us, length us, event | category | flops | bytes accessed | tf_op | source)
XLA Modules:
  0.0 61.8 jit_solution(18210416195266771235)
XLA Ops:
  0.0 0.0 copy-start
  0.0 1.1 %copy-done = bf16[1,512,768]{2,1,0:T(8,128)(2,1)S(1)} copy-done((bf16[1,512,768]{2,1,0:T(8,128)(2,1)S(1)}, bf16[1,512,768]{2,1,0:T(8,128)(2,1)}, u32[]{:S(2)}) %copy-start) | copy-done | bytes 786456
  1.1 0.0 copy-start.1
  1.1 0.7 %copy-done.1 = s32[1,512]{1,0:T(1,128)S(1)} copy-done((s32[1,512]{1,0:T(1,128)S(1)}, s32[1,512]{1,0:T(1,128)}, u32[]{:S(2)}) %copy-start.1) | copy-done | bytes 2072
  1.8 59.4 %shard_map.28 = f32[1,512]{1,0:T(1,128)S(1)} custom-call(bf16[1,512,768]{2,1,0:T(8,128)(2,1)S(1)} %copy-done, s32[1,512]{1,0:T(1,128)S(1)} %copy-done.1), custom_call_target="tpu_custom_call" | custom-call | flops 6845104128 | bytes 1048576 | tf_op jit(solution)/shard_map/pallas_call | solution.py:436
  61.2 0.6 copy.4
Async XLA Ops:
  0.0 1.1 %copy-start = (bf16[1,512,768]{2,1,0:T(8,128)(2,1)S(1)}, bf16[1,512,768]{2,1,0:T(8,128)(2,1)}, u32[]{:S(2)}) copy-start(bf16[1,512,768]{2,1,0:T(8,128)(2,1)} %x_ref.1) | copy-start | bytes 2359300
  1.1 0.7 %copy-start.1 = (s32[1,512]{1,0:T(1,128)S(1)}, s32[1,512]{1,0:T(1,128)}, u32[]{:S(2)}) copy-start(s32[1,512]{1,0:T(1,128)} %id_ref.1) | copy-start | bytes 6148

commit v4 on v3

--- a/solution.py
+++ b/solution.py
@@ -15,13 +15,12 @@
 COVER = ((0, 0), (0, 1), (0, -1), (1, -1), (-1, -1), (2, -1))
 SIBLING = (0, 1, 3)
 OFFSETS = (0, 1, -1, 2, -2, 3, -3, 4)
-FULL = ((0, 2), (0, 3), (0, 4), (2, 3), (2, 6), (1, 6), (4, 6), (4, 8), (0, 5), (5, 6), (5, 8))
-HALF = ((1, 2, 0), (1, 3, 0), (1, 4, 0), (0, 6, 2), (3, 6, 2), (3, 8, 2), (1, 7, 2), (1, 5, 0), (2, 5, 1))
+FULL = ((0, 2), (0, 3), (2, 3), (0, 4), (2, 6), (1, 6), (4, 6), (4, 8), (5, 0), (5, 6), (5, 8))
+HALF = ((1, 2, 0), (1, 4, 0), (0, 6, 2), (1, 3, 0), (3, 6, 2), (3, 8, 2), (1, 7, 2), (5, 1, 0), (5, 2, 1))
 EDGES = (
     (0, 1, (0, -1)), (0, 2, (0, 1)), (2, 3, (-1, 0)), (2, 4, (1, 0)), (3, 5, (-1, 0)), (4, 5, (1, 0)),
-    (0, 6, None), (1, 7, None), (3, 8, None), (2, 5, (2, 0)),
+    (0, 6, None), (1, 7, None), (3, 8, None),
 )
-DIRECT = 7
 
 
 def pick(n, table):
@@ -113,7 +112,7 @@
         )
 
     def edges_of(p):
-        return (0, 1, 2, 3, 9 if p >= DIRECT else 4 + p % 2, 6, 7, 8)
+        return (0, 1, 2, 3, 4 + p % 2, 6, 7, 8)
 
     def go(p, *edges):
         for e in edges:
@@ -132,7 +131,7 @@
 
     def into2(p):
         come(p, 1)
-        go(p, 2, 3, 9)
+        go(p, 2, 3)
 
     def into1(p):
         come(p, 0)
@@ -291,11 +290,11 @@
         score(i, j, (h, 256), (h, 256))
 
     def settle(slot):
-        best = jnp.max(colacc[slot], axis=0, keepdims=True) if slot != 1 else None
-        if slot < 6:
-            rows = jnp.max(rowacc[slot].T, axis=0, keepdims=True)
-            best = rows if best is None else jnp.maximum(best, rows)
-        res[slot] = best
+        res[slot] = jnp.max(rowacc[slot].T, axis=0, keepdims=True)
+
+    def finish(slot):
+        best = jnp.max(colacc[slot], axis=0, keepdims=True)
+        res[slot] = jnp.maximum(best, res[slot]) if slot < 6 else best
 
     def r_copy(slot):
         du, dv = COVER[slot] if slot < 6 else COVER[SIBLING[slot - 6]][::-1]
@@ -306,7 +305,7 @@
 
     def answer(*chosen):
         for slot in chosen:
-            settle(slot)
+            finish(slot)
             r_copy(slot).start()
 
     bounds_a()
@@ -351,7 +350,7 @@
     into3(4)
     into4(4)
     identify((3, 4, 5), ())
-    identify((), (0, 2, 3, 4, 5, 6, 7, 8))
+    identify((), (0, 1, 2, 3, 4, 6, 7, 8))
     into2(7)
     into4(5)
     loop(FULL[:4], early, 4)
@@ -372,29 +371,32 @@
     for p in range(4, 8):
         come(p, 6)
     loop(FULL[4:6], late, 2)
-    loop(HALF[3:4], half, 1)
+    loop(HALF[2:3], half, 1)
     into4(7)
-    loop(HALF[:1], half, 1)
+    loop(FULL[3:4], late, 1)
+    loop(FULL[6:7], late, 1)
+    loop(HALF[:2], half, 2)
     score(0, 0, (0, 256), (256, 256))
     score(0, 0, (256, 256), (256, 256), True)
     into3(7)
-    loop(FULL[1:4], late, 3)
-    loop(FULL[6:7], late, 1)
-    loop(HALF[1:3], half, 2)
-    loop(HALF[4:5], half, 1)
+    loop(FULL[1:3], late, 2)
+    loop(HALF[3:5], half, 2)
     for p in range(4, 8):
         come(p, 8)
     loop(FULL[7:8], late, 1)
     for p in range(8):
         come(p, 7)
     loop(HALF[5:7], half, 2)
+    for slot in (3, 4, 0, 1, 2):
+        settle(slot)
     answer(3, 4, 7)
     for p in range(4, 8):
-        come(p, 4, 5, 9)
+        come(p, 4, 5)
     loop(FULL[8:], late, 3)
     loop(HALF[7:], half, 2)
-    answer(5, 1, 2, 6, 8)
-    settle(0)
+    settle(5)
+    answer(5, 8, 1, 2, 6)
+    finish(0)
     bounds_end()
     for p in range(8):
         if p:
@@ -454,7 +456,7 @@
             pltpu.VMEM((8, 128), jnp.float32),
             pltpu.VMEM((4, 8, 128), jnp.float32),
             pltpu.VMEM((8, 128), jnp.int32),
-            dma((8,)), dma((8,)), dma((8,)), dma((10, 8)), dma((10, 8)), dma((9,)), dma((9,)), dma((8,)), dma((8,)),
+            dma((8,)), dma((8,)), dma((8,)), dma((9, 8)), dma((9, 8)), dma((9,)), dma((9,)), dma((8,)), dma((8,)),
             dma, dma((8,)), dma((8,)), dma, dma((4,)), dma((4,)),
         ],
         compiler_params=pltpu.CompilerParams(

time: 62 us -> 60.7 us (0.979)
  Pallas kernels: 59.4 us -> 58.1 us
    pallas_call x1, Pallas kernels: 59.4 us -> 58.1 us  [local(): pl.pallas_call(kernel, out_shape=jax.ShapeDtypeStruct((1, ROWS), jnp.floa...]
where the time goes in v4:
time: 60.7 us; the launch traced here: 60.5 us
  Pallas kernels  58.1 us (96%)
  local copies, waits for them, and re-layouts  2.39 us (4%)
    pallas_call x1, Pallas kernels, local(): pl.pallas_call(kernel, out_shape=jax.ShapeDtypeStruct((1, ROWS), jnp.floa...  58.1 us
    unnamed x5, local copies, waits for them, and re-layouts  2.39 us

profile of v4, /device:TPU:24, one launch (start us, length us, event | category | flops | bytes accessed | tf_op | source)
XLA Modules:
  0.0 60.5 jit_solution(17963083567337088762)
XLA Ops:
  0.0 0.0 copy-start
  0.0 1.1 %copy-done = bf16[1,512,768]{2,1,0:T(8,128)(2,1)S(1)} copy-done((bf16[1,512,768]{2,1,0:T(8,128)(2,1)S(1)}, bf16[1,512,768]{2,1,0:T(8,128)(2,1)}, u32[]{:S(2)}) %copy-start) | copy-done | bytes 786456
  1.1 0.0 copy-start.1
  1.1 0.7 %copy-done.1 = s32[1,512]{1,0:T(1,128)S(1)} copy-done((s32[1,512]{1,0:T(1,128)S(1)}, s32[1,512]{1,0:T(1,128)}, u32[]{:S(2)}) %copy-start.1) | copy-done | bytes 2072
  1.8 58.1 %shard_map.28 = f32[1,512]{1,0:T(1,128)S(1)} custom-call(bf16[1,512,768]{2,1,0:T(8,128)(2,1)S(1)} %copy-done, s32[1,512]{1,0:T(1,128)S(1)} %copy-done.1), custom_call_target="tpu_custom_call" | custom-call | flops 6845104128 | bytes 1048576 | tf_op jit(solution)/shard_map/pallas_call | solution.py:438
  59.9 0.6 copy.4
Async XLA Ops:
  0.0 1.1 %copy-start = (bf16[1,512,768]{2,1,0:T(8,128)(2,1)S(1)}, bf16[1,512,768]{2,1,0:T(8,128)(2,1)}, u32[]{:S(2)}) copy-start(bf16[1,512,768]{2,1,0:T(8,128)(2,1)} %x_ref.1) | copy-start | bytes 2359300
  1.1 0.7 %copy-start.1 = (s32[1,512]{1,0:T(1,128)S(1)}, s32[1,512]{1,0:T(1,128)}, u32[]{:S(2)}) copy-start(s32[1,512]{1,0:T(1,128)} %id_ref.1) | copy-start | bytes 6148

commit v5 on v4

--- a/solution.py
+++ b/solution.py
@@ -343,16 +343,16 @@
     into2(5)
     into4(3)
     into3(3)
-    bounds_d()
-    identify((0, 1, 2), ())
     into2(6)
     into1(5)
     into3(4)
     into4(4)
+    bounds_d()
+    identify((0, 1, 2), ())
+    into2(7)
+    into4(5)
     identify((3, 4, 5), ())
     identify((), (0, 1, 2, 3, 4, 6, 7, 8))
-    into2(7)
-    into4(5)
     loop(FULL[:4], early, 4)
     into1(7)
     loop(FULL[:1], late, 1)

time: 60.7 us -> 60.7 us (level)
  no operation moved by 1% of the time
where the time goes in v5:
time: 60.7 us; the launch traced here: 60.5 us
  Pallas kernels  58.1 us (96%)
  local copies, waits for them, and re-layouts  2.39 us (4%)
    pallas_call x1, Pallas kernels, local(): pl.pallas_call(kernel, out_shape=jax.ShapeDtypeStruct((1, ROWS), jnp.floa...  58.1 us
    unnamed x5, local copies, waits for them, and re-layouts  2.39 us

profile of v5, /device:TPU:24, one launch (start us, length us, event | category | flops | bytes accessed | tf_op | source)
XLA Modules:
  0.0 60.5 jit_solution(9154659440052793153)
XLA Ops:
  0.0 0.0 copy-start
  0.0 1.1 %copy-done = bf16[1,512,768]{2,1,0:T(8,128)(2,1)S(1)} copy-done((bf16[1,512,768]{2,1,0:T(8,128)(2,1)S(1)}, bf16[1,512,768]{2,1,0:T(8,128)(2,1)}, u32[]{:S(2)}) %copy-start) | copy-done | bytes 786456
  1.1 0.0 copy-start.1
  1.1 0.7 %copy-done.1 = s32[1,512]{1,0:T(1,128)S(1)} copy-done((s32[1,512]{1,0:T(1,128)S(1)}, s32[1,512]{1,0:T(1,128)}, u32[]{:S(2)}) %copy-start.1) | copy-done | bytes 2072
  1.8 58.1 %shard_map.28 = f32[1,512]{1,0:T(1,128)S(1)} custom-call(bf16[1,512,768]{2,1,0:T(8,128)(2,1)S(1)} %copy-done, s32[1,512]{1,0:T(1,128)S(1)} %copy-done.1), custom_call_target="tpu_custom_call" | custom-call | flops 6845104128 | bytes 1048576 | tf_op jit(solution)/shard_map/pallas_call | solution.py:438
  59.9 0.6 copy.4
Async XLA Ops:
  0.0 1.1 %copy-start = (bf16[1,512,768]{2,1,0:T(8,128)(2,1)S(1)}, bf16[1,512,768]{2,1,0:T(8,128)(2,1)}, u32[]{:S(2)}) copy-start(bf16[1,512,768]{2,1,0:T(8,128)(2,1)} %x_ref.1) | copy-start | bytes 2359300
  1.1 0.7 %copy-start.1 = (s32[1,512]{1,0:T(1,128)S(1)}, s32[1,512]{1,0:T(1,128)}, u32[]{:S(2)}) copy-start(s32[1,512]{1,0:T(1,128)} %id_ref.1) | copy-start | bytes 6148
